TPU v7x, 256 devices: a whole 4x4x8 slice. The times are simulated.
256 devices in a mesh: prow: 16 (over x, y), pcol: 16 (over z, core).
Axes of the slice: x: 4, y: 4, z: 8, core: 2. Of those that a mesh axis runs over, the one named last changes fastest.
Arguments:
- inverse_tiles: float32 [24576, 24576], P('prow', 'pcol'), may hold values from -6 to 6
- factor_rows: float32 [24576, 512], P('prow'), may hold values from -0.0390625 to 0.0390625
- diag_inverse: float32 [512, 512], P('prow', 'pcol'), may hold values from -6 to 6
- pattern: int32 [192], replicated, may hold values from 0 to 1, as said below
Outputs:
- column_block: float32 [24576, 512], P(('prow', 'pcol'))
- diagonal_block: float32 [512, 512], P('prow', 'pcol')
Inputs may be any that keep to these rules, and one draw needn't show every extreme that they name: `pattern`: 1 where the block of ancestor rows lies in the supernode's structure, else 0; the first block always lies in it and the last never.
All inputs are finite; a program needn't handle non-finite values.
Results may differ from a plain program's by a relative error of at most 0.000078.
Values sent between devices are 32-bit elements; how exact they have to be, the bound alone decides.
A program may use at most 64 MiB of HBM per device.

v0:
```python
import jax
import jax.numpy as jnp
from jax import lax
from jax.sharding import PartitionSpec as P

BLK = 128


def broadcast(shard, axis, root):
    mine = lax.axis_index(axis) == root
    return lax.psum(jnp.where(mine, shard, jnp.zeros_like(shard)), axis)


def row_select(pattern, first_row, row_count):
    global_rows = first_row + lax.iota(jnp.int32, row_count)
    block_ids = global_rows // BLK
    blocks = lax.iota(jnp.int32, pattern.shape[0])
    match = block_ids[:, None] == blocks[None, :]
    return jnp.sum(jnp.where(match, pattern[None, :], 0), axis=1).astype(jnp.float32)


def local(inverse_tiles, factor_rows, diag_inverse, pattern):
    n_row = lax.axis_size("prow")
    n_col = lax.axis_size("pcol")
    row_index = lax.axis_index("prow")
    col_index = lax.axis_index("pcol")
    tile_rows = inverse_tiles.shape[0]
    width = factor_rows.shape[1]
    col_ratio = n_col // n_row
    tile_mask = row_select(pattern, row_index * tile_rows, tile_rows)
    masked_rows = factor_rows * tile_mask[:, None]
    root_index = col_index // col_ratio
    column_factor = broadcast(masked_rows, "prow", root_index)
    out_rows = tile_rows // n_col
    own_mask = lax.dynamic_slice_in_dim(tile_mask, col_index * out_rows, out_rows, 0)
    summed = lax.psum_scatter(
        jnp.dot(
            inverse_tiles,
            column_factor,
            precision=lax.Precision.HIGHEST,
            preferred_element_type=jnp.float32,
        ),
        "pcol",
        scatter_dimension=0,
        tiled=True,
    )
    column_block = -summed * own_mask[:, None]
    own_factor = lax.dynamic_slice_in_dim(masked_rows, col_index * out_rows, out_rows, 0)
    correction = jnp.dot(
        own_factor.T,
        column_block,
        precision=lax.Precision.HIGHEST,
        preferred_element_type=jnp.float32,
    )
    share_rows = width // n_row
    share_cols = width // n_col
    total = lax.psum(correction, ("prow", "pcol"))
    mine = lax.dynamic_slice_in_dim(total, row_index * share_rows, share_rows, 0)
    mine = lax.dynamic_slice_in_dim(mine, col_index * share_cols, share_cols, 1)
    diagonal_block = diag_inverse - mine
    return (column_block, diagonal_block)


def solution(mesh):
    return jax.shard_map(
        local,
        mesh=mesh,
        in_specs=(P("prow", "pcol"), P("prow", None), P("prow", "pcol"), P()),
        out_specs=(P(("prow", "pcol"), None), P("prow", "pcol")),
        check_vma=False,
    )
```

profile of v0, /device:TPU:2, one launch (start us, length us, event | category | flops | bytes accessed | tf_op | source)
XLA Modules:
  0.0 486.7 jit_solution(2618782349382456584)
XLA Ops:
  7.2 0.0 all-reduce.3.cloned.1.call-start
  7.2 0.9 select_reduce_fusion
  8.2 4.1 broadcast_select_fusion
  12.2 0.0 all-reduce.3.cloned.1.call-update
  12.3 0.0 reduce-scatter.4.cloned.1.call-start
  12.3 108.1 %all-reduce.3.cloned.1.call-done = f32[1536,512]{1,0:T(8,128)} async-done(((f32[1536,512]{1,0:T(8,128)}), f32[1536,512]{1,0:T(8,128)}) %all-reduce.3.cloned.1.call-update) | async-done | bytes 3145744 | tf_op jit(solution)/shard_map/psum | solution.py:11
  120.4 33.8 %convolution_bitcast_fusion = f32[1536,512]{0,1:T(8,128)} fusion(f32[1536,512]{1,0:T(8,128)} %all-reduce.3.cloned.1.call-done, f32[1536,1536]{1,0:T(8,128)} %param.4), kind=kOutput, calls=%fused_computation | convolution fusion | flops 14495514624 | bytes 15728640 | tf_op jit(solution)/shard_map/dot_general | solution.py:37
  154.1 3.5 copy.9
  157.7 0.0 copy-start
  157.7 0.0 reduce-scatter.4.cloned.1.call-update
  157.7 0.0 all-reduce.5.cloned.1.call-start
  157.8 0.1 dynamic_slice.10
  157.9 61.0 %reduce-scatter.4.cloned.1.call-done = f32[96,512]{1,0:T(8,128)} async-done(((f32[1536,512]{1,0:T(8,128)}), f32[96,512]{1,0:T(8,128)}) %reduce-scatter.4.cloned.1.call-update) | async-done | bytes 196624
  218.8 1.8 copy.10
  220.6 1.0 negate_multiply_fusion
  221.6 2.1 fusion
  223.6 0.0 all-reduce.5.cloned.1.call-update
  223.7 0.8 copy.8
  224.5 254.3 %all-reduce.5.cloned.1.call-done = f32[512,512]{1,0:T(8,128)} async-done(((f32[512,512]{1,0:T(8,128)}), f32[512,512]{1,0:T(8,128)}) %all-reduce.5.cloned.1.call-update) | async-done | bytes 1048592 | tf_op jit(solution)/shard_map/psum | solution.py:57
  478.8 0.0 copy-done
  478.8 1.5 dynamic-slice_subtract_fusion
  (2 shorter events, 0.0 us)
Async XLA Ops:
  7.2 113.2 %all-reduce.3.cloned.1.call-start = ((), (), s32[]{:S(2)}) async-start(), calls=%async_computation.1 | async-start | bytes 6291456 | tf_op jit(solution)/shard_map/psum | solution.py:11
  12.3 206.6 %reduce-scatter.4.cloned.1.call-start = ((), (), s32[]{:S(2)}) async-start(), calls=%async_computation.3 | async-start | bytes 3342336
  157.7 321.1 %copy-start = (f32[32,32]{1,0:T(8,128)S(1)}, f32[32,32]{1,0:T(8,128)}, u32[]{:S(2)}) copy-start(f32[32,32]{1,0:T(8,128)} %param.6) | copy-start | bytes 12292
  157.7 321.0 %all-reduce.5.cloned.1.call-start = ((), (), s32[]{:S(2)}) async-start(), calls=%async_computation.2 | async-start | bytes 2097152 | tf_op jit(solution)/shard_map/psum | solution.py:57
Sparse Core Ops, SparseCore 0:
  12.4 107.9 all-reduce.2
  157.8 60.9 reduce-scatter.3
  224.3 254.4 all-reduce.4
where the time goes:
time: 487 us
  waiting for transfers between devices  423 us (87%)
  matrix products  35.8 us (7%)
  between operations  13.8 us (3%)
  other arithmetic  7.43 us (2%)
  local copies, waits for them, and re-layouts  6.18 us (1%)
    psum x1, waiting for transfers between devices, local(): total = lax.psum(correction, ('prow', 'pcol'))  254 us
    psum x1, waiting for transfers between devices, broadcast(): return lax.psum(jnp.where(mine, shard, jnp.zeros_like(shard)), axis)  108 us
    unnamed x4, waiting for transfers between devices  61 us
    dot_general x1, matrix products, local(): jnp.dot(inverse_tiles, column_factor, precision=lax.Precision.HIGHEST, pr...  33.8 us
  transfers between devices with their start and end apart: 3, of which 3 were waited for; matrix products, arithmetic and copies ran while one was open for 0% of the time, Pallas kernels for 0%

commit v1 on v0

--- a/solution.py
+++ b/solution.py
@@ -54,7 +54,7 @@
     )
     share_rows = width // n_row
     share_cols = width // n_col
-    total = lax.psum(correction, ("prow", "pcol"))
+    total = lax.psum(lax.psum(correction, "pcol"), "prow")
     mine = lax.dynamic_slice_in_dim(total, row_index * share_rows, share_rows, 0)
     mine = lax.dynamic_slice_in_dim(mine, col_index * share_cols, share_cols, 1)
     diagonal_block = diag_inverse - mine

time: 487 us -> 443 us (0.910)
  waiting for transfers between devices: 423 us -> 379 us
    psum x1 -> x2, waiting for transfers between devices: 254 us -> 210 us  [local(): total = lax.psum(lax.psum(correction, 'pcol'), 'prow')]
    unnamed x4 -> x5, waiting for transfers between devices: 61 us -> 61 us
  transfers between devices with their start and end apart: 3 -> 4, of which waited for: 3 -> 4; matrix products, arithmetic and copies ran while one was open for 0% -> 0% of each run, Pallas kernels for 0% -> 0%
where the time goes in v1:
time: 443 us; the launch traced here: 442 us
  waiting for transfers between devices  379 us (86%)
  matrix products  35.8 us (8%)
  between operations  13.8 us (3%)
  other arithmetic  7.43 us (2%)
  local copies, waits for them, and re-layouts  6.19 us (1%)
    psum x2, waiting for transfers between devices, local(): total = lax.psum(lax.psum(correction, 'pcol'), 'prow')  210 us
    psum x1, waiting for transfers between devices, broadcast(): return lax.psum(jnp.where(mine, shard, jnp.zeros_like(shard)), axis)  108 us
    unnamed x5, waiting for transfers between devices  61 us
    dot_general x1, matrix products, local(): jnp.dot(inverse_tiles, column_factor, precision=lax.Precision.HIGHEST, pr...  33.8 us
  transfers between devices with their start and end apart: 4, of which 4 were waited for; matrix products, arithmetic and copies ran while one was open for 0% of the time, Pallas kernels for 0%

profile of v1, /device:TPU:2, one launch (start us, length us, event | category | flops | bytes accessed | tf_op | source)
XLA Modules:
  0.0 442.3 jit_solution(2130751619566210688)
XLA Ops:
  7.2 0.0 all-reduce.4.cloned.1.call-start
  7.2 0.9 select_reduce_fusion
  8.2 4.1 broadcast_select_fusion
  12.2 0.0 all-reduce.4.cloned.1.call-update
  12.3 0.0 reduce-scatter.4.cloned.1.call-start
  12.3 108.1 %all-reduce.4.cloned.1.call-done = f32[1536,512]{1,0:T(8,128)} async-done(((f32[1536,512]{1,0:T(8,128)}), f32[1536,512]{1,0:T(8,128)}) %all-reduce.4.cloned.1.call-update) | async-done | bytes 3145744 | tf_op jit(solution)/shard_map/psum | solution.py:11
  120.4 33.8 %convolution_bitcast_fusion = f32[1536,512]{0,1:T(8,128)} fusion(f32[1536,512]{1,0:T(8,128)} %all-reduce.4.cloned.1.call-done, f32[1536,1536]{1,0:T(8,128)} %param.4), kind=kOutput, calls=%fused_computation | convolution fusion | flops 14495514624 | bytes 15728640 | tf_op jit(solution)/shard_map/dot_general | solution.py:37
  154.1 3.5 copy.9
  157.7 0.0 reduce-scatter.4.cloned.1.call-update
  157.7 0.0 copy-start
  157.7 0.0 all-reduce.6.cloned.1.call-start
  157.8 0.1 dynamic_slice.10
  157.9 61.0 %reduce-scatter.4.cloned.1.call-done = f32[96,512]{1,0:T(8,128)} async-done(((f32[1536,512]{1,0:T(8,128)}), f32[96,512]{1,0:T(8,128)}) %reduce-scatter.4.cloned.1.call-update) | async-done | bytes 196624
  218.8 1.8 copy.10
  220.6 1.0 negate_multiply_fusion
  221.6 2.1 fusion
  223.6 0.0 all-reduce.6.cloned.1.call-update
  223.7 0.0 all-reduce.8.cloned.1.call-start
  223.7 110.2 %all-reduce.6.cloned.1.call-done = f32[512,512]{1,0:T(8,128)} async-done(((f32[512,512]{1,0:T(8,128)}), f32[512,512]{1,0:T(8,128)}) %all-reduce.6.cloned.1.call-update) | async-done | bytes 1048592 | tf_op jit(solution)/shard_map/psum | solution.py:57
  333.9 0.0 all-reduce.8.cloned.1.call-update
  333.9 0.8 copy.8
  334.8 99.6 %all-reduce.8.cloned.1.call-done = f32[512,512]{1,0:T(8,128)} async-done(((f32[512,512]{1,0:T(8,128)}), f32[512,512]{1,0:T(8,128)}) %all-reduce.8.cloned.1.call-update) | async-done | bytes 1048592 | tf_op jit(solution)/shard_map/psum | solution.py:57
  434.3 0.0 copy-done
  434.3 1.5 dynamic-slice_subtract_fusion
  (2 shorter events, 0.0 us)
Async XLA Ops:
  7.2 113.2 %all-reduce.4.cloned.1.call-start = ((), (), s32[]{:S(2)}) async-start(), calls=%async_computation.1 | async-start | bytes 6291456 | tf_op jit(solution)/shard_map/psum | solution.py:11
  12.3 206.6 %reduce-scatter.4.cloned.1.call-start = ((), (), s32[]{:S(2)}) async-start(), calls=%async_computation.4 | async-start | bytes 3342336
  157.7 276.6 %copy-start = (f32[32,32]{1,0:T(8,128)S(1)}, f32[32,32]{1,0:T(8,128)}, u32[]{:S(2)}) copy-start(f32[32,32]{1,0:T(8,128)} %param.6) | copy-start | bytes 12292
  157.7 176.2 %all-reduce.6.cloned.1.call-start = ((), (), s32[]{:S(2)}) async-start(), calls=%async_computation.2 | async-start | bytes 2097152 | tf_op jit(solution)/shard_map/psum | solution.py:57
  223.7 210.7 %all-reduce.8.cloned.1.call-start = ((), (), s32[]{:S(2)}) async-start(), calls=%async_computation.3 | async-start | bytes 2097152 | tf_op jit(solution)/shard_map/psum | solution.py:57
Sparse Core Ops, SparseCore 0:
  12.4 107.9 all-reduce.3
  157.8 60.9 reduce-scatter.3
  223.8 110.0 all-reduce.5
  337.4 96.9 all-reduce.7
